TPU v7x, 32 devices: a whole 2x2x4 slice. The times are simulated.
32 devices in a mesh: gx: 2 (over x), gy: 4 (over y, core), gz: 4 (over z).
Axes of the slice: x: 2, y: 2, z: 4, core: 2. Of those that a mesh axis runs over, the one named last changes fastest.
Arguments:
- charges: float32 [128, 1024, 256], P('gz', 'gy', 'gx'), may hold values from -8 to 8
- fine_taps: float32 [2, 3, 17], replicated, may hold values from 0.05 to 0.45
- coarse_taps: float32 [2, 3, 17], replicated, may hold values from 0.05 to 0.45
Outputs:
- potential: float32 [128, 1024, 256], P('gz', 'gy', 'gx')
All inputs are finite; a program needn't handle non-finite values.
Results may differ from a plain program's by a relative error of at most 0.0003.
Values sent between devices are 32-bit elements; how exact they have to be, the bound alone decides.
A program may use at most 128 MiB of HBM per device.

v0:
```python
import functools

import jax
import jax.numpy as jnp
from jax import lax
from jax.experimental import pallas as pl
from jax.experimental.pallas import tpu as pltpu
from jax.sharding import PartitionSpec as P

RADIUS = 8
TOPB = 16
AXES = ("gz", "gy", "gx")
precise = lax.Precision.HIGHEST
f32, bf16 = jnp.float32, jnp.bfloat16


def shift(block, axis, by):
    n = lax.axis_size(axis)
    return lax.ppermute(block, axis, [(i, (i + by) % n) for i in range(n)])


def split(mat):
    high = lax.reduce_precision(mat, 8, 7)
    return high.astype(bf16), (mat - high).astype(bf16)


def split_in(val):
    high = val.astype(bf16)
    return high, (val - high.astype(f32)).astype(bf16)


def mm(a, b, dims=((1,), (0,))):
    return lax.dot_general(a, b, (dims, ((), ())), preferred_element_type=f32)


def mm3(a, b, dims=((1,), (0,))):
    return mm(a[0], b[0], dims) + mm(a[1], b[0], dims) + mm(a[0], b[1], dims)


def band(taps, length_in, length_out, repeat=1):
    spread = taps.shape[1]
    diff = (
        jnp.arange(length_in, dtype=jnp.int32)[:, None]
        - jnp.arange(length_out * repeat, dtype=jnp.int32)[None, :] // repeat
    )
    out = jnp.zeros((taps.shape[0],) + diff.shape, f32)
    for k in range(spread):
        out = jnp.where(diff[None] == k, taps[:, k, None, None], out)
    return out


def xy_kernel(planes, size_y, size_x, c_ref, ylo_ref, yhi_ref, xs_ref,
              bmh, bml, beh, bel, byh, byl, g_ref):
    ext_y = size_y + 2 * RADIUS
    rows = jnp.concatenate(
        [part for p in range(planes) for part in (ylo_ref[p], c_ref[p], yhi_ref[p])], axis=0
    )
    mid = mm3(split_in(rows), (bmh[...], bml[...]))
    parts = []
    for p in range(planes):
        edge = mm3(split_in(xs_ref[p]), (beh[...], bel[...]), ((0,), (0,)))
        parts.append(mid[p * ext_y:(p + 1) * ext_y] + edge)
    for t in range(2):
        right = jnp.concatenate([part[:, t * size_x:(t + 1) * size_x] for part in parts], axis=1)
        out = mm3((byh[t], byl[t]), split_in(right))
        for p in range(planes):
            g_ref[t, p] = out[:, p * size_x:(p + 1) * size_x]


def xy_pass(block, ylo, yhi, xs, mats):
    size_z, size_y, size_x = block.shape
    planes = 4
    whole = lambda a: pl.BlockSpec(a.shape, lambda i: (0,) * a.ndim)
    lead = lambda a: pl.BlockSpec((planes,) + a.shape[1:], lambda i: (i, 0, 0))
    return pl.pallas_call(
        functools.partial(xy_kernel, planes, size_y, size_x),
        grid=(size_z // planes,),
        in_specs=[lead(a) for a in (block, ylo, yhi, xs)] + [whole(m) for m in mats],
        out_specs=pl.BlockSpec((2, planes, size_y, size_x), lambda i: (0, i, 0, 0)),
        out_shape=jax.ShapeDtypeStruct((2, size_z, size_y, size_x), f32),
        compiler_params=pltpu.CompilerParams(vmem_limit_bytes=40 * 2**20),
        cost_estimate=pl.CostEstimate(
            flops=size_z * 2 * 600 * 10**6 // 10, bytes_accessed=3 * block.size * 4, transcendentals=0
        ),
    )(block, ylo, yhi, xs, *mats)


def z_own_kernel(size_z, groups, w_ref, g_ref, e_ref, o_ref):
    def body(r, carry):
        rows = pl.ds(pl.multiple_of(r * 8, 8), 8)
        acc = [e_ref[o // 2, rows, :] for o in range(size_z)]
        for t in range(2):
            for z in range(size_z):
                val = g_ref[t, z, rows, :]
                for o in range(max(0, z - RADIUS), min(size_z, z + RADIUS + 1)):
                    acc[o] = acc[o] + w_ref[t, z - o + RADIUS] * val
        for o in range(size_z):
            o_ref[o, rows, :] = acc[o]
        return carry

    lax.fori_loop(0, groups, body, 0)


def z_own(taps_z, g, expanded):
    _, size_z, size_y, size_x = g.shape
    blk = 32
    return pl.pallas_call(
        functools.partial(z_own_kernel, size_z, blk // 8),
        grid=(size_y // blk,),
        in_specs=[
            pl.BlockSpec(memory_space=pltpu.SMEM),
            pl.BlockSpec((2, size_z, blk, size_x), lambda i: (0, 0, i, 0)),
            pl.BlockSpec((size_z // 2, blk, size_x), lambda i: (0, i, 0)),
        ],
        out_specs=pl.BlockSpec((size_z, blk, size_x), lambda i: (0, i, 0)),
        out_shape=jax.ShapeDtypeStruct((size_z, size_y, size_x), f32),
        compiler_params=pltpu.CompilerParams(vmem_limit_bytes=40 * 2**20),
        cost_estimate=pl.CostEstimate(flops=10**10, bytes_accessed=5 * g.size, transcendentals=0),
    )(taps_z, g, expanded)


def z_halo_kernel(groups, w_ref, g_ref, p_ref, o_ref):
    def side(high):
        def body(r, carry):
            rows = pl.ds(pl.multiple_of(r * 8, 8), 8)
            acc = [p_ref[o, rows, :] for o in range(RADIUS)]
            for t in range(2):
                for z in range(RADIUS):
                    val = g_ref[t, z, rows, :]
                    for o in range(RADIUS):
                        off = z + RADIUS - o if high else z - RADIUS - o
                        if -RADIUS <= off <= RADIUS:
                            acc[o] = acc[o] + w_ref[t, off + RADIUS] * val
            for o in range(RADIUS):
                o_ref[o, rows, :] = acc[o]
            return carry

        lax.fori_loop(0, groups, body, 0)

    @pl.when(pl.program_id(0) == 0)
    def _():
        side(False)

    @pl.when(pl.program_id(0) == 1)
    def _():
        side(True)


def z_halo(taps_z, g_halo, partial):
    size_z, size_y, size_x = partial.shape
    blk = min(size_y, 128)
    last = size_z // RADIUS - 1
    spot = pl.BlockSpec((RADIUS, blk, size_x), lambda s, i: (s * last, i, 0))
    return pl.pallas_call(
        functools.partial(z_halo_kernel, blk // 8),
        grid=(2, size_y // blk),
        in_specs=[
            pl.BlockSpec(memory_space=pltpu.SMEM),
            pl.BlockSpec((2, RADIUS, blk, size_x), lambda s, i: (0, s, i, 0)),
            spot,
        ],
        out_specs=spot,
        out_shape=jax.ShapeDtypeStruct(partial.shape, f32),
        input_output_aliases={2: 0},
        compiler_params=pltpu.CompilerParams(vmem_limit_bytes=40 * 2**20),
    )(taps_z, g_halo, partial)


def pool_kernel(planes, c_ref, py_ref, px_ref, o_ref):
    for p in range(planes):
        both = c_ref[2 * p] + c_ref[2 * p + 1]
        high, low = split_in(both)
        along_x = mm(high, px_ref[...]) + mm(low, px_ref[...])
        high, low = split_in(along_x)
        o_ref[p] = mm(py_ref[...], high) + mm(py_ref[...], low)


def pool(block):
    size_z, size_y, size_x = block.shape
    planes = 4
    pick = lambda n, w: ((jnp.arange(n)[:, None] // 2 == jnp.arange(n // 2)[None, :]) * w).astype(bf16)
    px, py = pick(size_x, 0.5), pick(size_y, 0.25).T
    return pl.pallas_call(
        functools.partial(pool_kernel, planes),
        grid=(size_z // (2 * planes),),
        in_specs=[
            pl.BlockSpec((2 * planes, size_y, size_x), lambda i: (i, 0, 0)),
            pl.BlockSpec(py.shape, lambda i: (0, 0)),
            pl.BlockSpec(px.shape, lambda i: (0, 0)),
        ],
        out_specs=pl.BlockSpec((planes, size_y // 2, size_x // 2), lambda i: (i, 0, 0)),
        out_shape=jax.ShapeDtypeStruct((size_z // 2, size_y // 2, size_x // 2), f32),
    )(block, py, px)


def coarse_kernel(planes, w_ref, ext_ref, top_ref, bxh, bxl, byh, byl, o_ref):
    first = pl.program_id(0) * planes
    for p in range(planes):
        total = top_ref[0]
        sums = [0.0, 0.0]
        for k in range(2 * RADIUS + 1):
            val = ext_ref[first + p + k]
            for t in range(2):
                sums[t] = sums[t] + w_ref[t, k] * val
        for t in range(2):
            along_x = mm3(split_in(sums[t]), (bxh[t], bxl[t]))
            total = total + mm3((byh[t], byl[t]), split_in(along_x))
        o_ref[p] = total


def coarse_level(ext, taps, top_wide, size_z, size_y, size_x):
    planes = 2
    bx = split(band(taps[:, 0], size_x + 2 * RADIUS, size_x, 2))
    by = split(band(taps[:, 1], size_y + 2 * RADIUS, size_y, 2).transpose(0, 2, 1))
    mats = bx + by
    whole = lambda a: pl.BlockSpec(a.shape, lambda i: (0,) * a.ndim)
    return pl.pallas_call(
        functools.partial(coarse_kernel, planes),
        grid=(size_z // planes,),
        in_specs=[
            pl.BlockSpec(memory_space=pltpu.SMEM),
            whole(ext),
            pl.BlockSpec((1,) + top_wide.shape[1:], lambda i: (i * planes // TOPB, 0, 0)),
        ] + [whole(m) for m in mats],
        out_specs=pl.BlockSpec((planes, 2 * size_y, 2 * size_x), lambda i: (i, 0, 0)),
        out_shape=jax.ShapeDtypeStruct((size_z, 2 * size_y, 2 * size_x), f32),
        compiler_params=pltpu.CompilerParams(vmem_limit_bytes=40 * 2**20),
        cost_estimate=pl.CostEstimate(flops=10**10, bytes_accessed=10**7, transcendentals=0),
    )(taps[:, 2], ext, top_wide, *mats)


def coarse_halo(coarse):
    size_z, size_y, size_x = coarse.shape
    r = RADIUS
    face = (r, size_y * size_x // 128, 128)
    low = shift(coarse[-r:].reshape(face), "gz", 1).reshape(r, size_y, size_x)
    high = shift(coarse[:r].reshape(face), "gz", -1).reshape(r, size_y, size_x)
    ext = jnp.concatenate([low, coarse, high], axis=0)
    low = shift(ext[:, -r:], "gy", 1)
    high = shift(ext[:, :r], "gy", -1)
    ext = jnp.concatenate([low, ext, high], axis=1)
    low = shift(ext[:, :, -r:].transpose(0, 2, 1), "gx", 1).transpose(0, 2, 1)
    high = shift(ext[:, :, :r].transpose(0, 2, 1), "gx", -1).transpose(0, 2, 1)
    return jnp.concatenate([low, ext, high], axis=2)


def top_wide_field(coarse):
    size_z, size_y, size_x = coarse.shape
    nz, ny, nx = size_z // TOPB, size_y // TOPB, size_x // TOPB
    along_z = coarse.reshape(nz, TOPB, size_y, size_x).sum(axis=1)
    block_of = lambda n: (jnp.arange(n)[:, None] // TOPB == jnp.arange(n // TOPB)[None, :]).astype(f32)
    grid = jnp.einsum("zyx,yj,xi->zji", along_z, block_of(size_y), block_of(size_x), precision=precise)
    field = grid.reshape(1, nz * ny * nx)
    counts = []
    for axis in ("gx", "gy", "gz"):
        n = lax.axis_size(axis)
        counts.append(n)
        field = jnp.stack([field] + [shift(field, axis, s) for s in range(1, n)], axis=0)
        field = field.reshape(-1, nz * ny * nx)
    field = field.reshape(counts[2], counts[1], counts[0], nz, ny, nx)

    def apart(count, n):
        total = count * n
        place = -jnp.arange(count, dtype=jnp.int32)[:, None] * n + jnp.arange(n, dtype=jnp.int32)[None, :]
        dist = jnp.arange(n, dtype=jnp.int32)[:, None, None] - place[None]
        dist = dist % total
        near = jnp.minimum(dist, total - dist).astype(f32)
        return near * near

    dz, dy, dx = apart(counts[2], nz), apart(counts[1], ny), apart(counts[0], nx)
    square = (
        1.0
        + dz[:, None, None, :, None, None, :, None, None]
        + dy[None, :, None, None, :, None, None, :, None]
        + dx[None, None, :, None, None, :, None, None, :]
    )
    weights = (1.0 / (TOPB * TOPB * jnp.sqrt(square))).reshape(nz * ny * nx, -1)
    out = jnp.dot(weights, field.reshape(-1), precision=precise).reshape(nz, ny, nx)
    wide = lambda n: (jnp.arange(n)[:, None] == jnp.arange(n * TOPB * 2)[None, :] // (TOPB * 2)).astype(f32)
    return jnp.einsum("zyx,yj,xi->zji", out, wide(ny), wide(nx), precision=precise)


def sides(block):
    r = RADIUS
    ylo = shift(block[:, -r:], "gy", 1)
    yhi = shift(block[:, :r], "gy", -1)

    def turned(cols):
        strip = jnp.concatenate([ylo[:, :, cols], block[:, :, cols], yhi[:, :, cols]], axis=1)
        return strip.transpose(0, 2, 1)

    xlo = shift(turned(slice(-r, None)), "gx", 1)
    xhi = shift(turned(slice(0, r)), "gx", -1)
    return ylo, yhi, jnp.concatenate([xlo, xhi], axis=1)


def on_device(charges, fine_taps, coarse_taps):
    size_z, size_y, size_x = charges.shape
    r = RADIUS
    zlo = shift(charges[-r:], "gz", 1)
    zhi = shift(charges[:r], "gz", -1)

    band_x = band(fine_taps[:, 0], size_x + 2 * r, size_x)
    band_x = jnp.concatenate([band_x[0], band_x[1]], axis=1)
    edge_x = jnp.concatenate([band_x[:r], band_x[-r:]], axis=0)
    band_y = band(fine_taps[:, 1], size_y + 2 * r, size_y).transpose(0, 2, 1)
    mats = split(band_x[r:-r]) + split(edge_x) + split(band_y)
    taps_z = fine_taps[:, 2]

    g_own = xy_pass(charges, *sides(charges), mats)
    coarse = pool(charges)
    top_wide = top_wide_field(coarse)
    ext = coarse_halo(coarse)
    expanded = coarse_level(ext, coarse_taps, top_wide, *coarse.shape)
    partial = z_own(taps_z, g_own, expanded)

    halo = jnp.concatenate([zlo, zhi], axis=0)
    g_halo = xy_pass(halo, *sides(halo), mats)
    return z_halo(taps_z, g_halo, partial)


def solution(mesh):
    return jax.shard_map(
        on_device,
        mesh=mesh,
        in_specs=(P("gz", "gy", "gx"), P(), P()),
        out_specs=P("gz", "gy", "gx"),
        check_vma=False,
    )
```

profile of v0, /device:TPU:0, one launch (start us, length us, event | category | flops | bytes accessed | tf_op | source)
XLA Modules:
  0.0 216.1 jit_solution(18202536882862663243)
XLA Ops:
  1.3 5.2 %shard_map.39 = f32[16,128,64]{2,1,0:T(8,128)} custom-call(f32[32,256,128]{2,1,0:T(8,128)} %c_ref.3, bf16[128,256]{1,0:T(8,128)(2,1)} %select_convert_fusion.py_ref, bf16[128,64]{1,0:T(8,128)(2,1)} %select_convert_fusion.1.px_ref), custom_call_target="tpu_custom_call" | custom-call | tf_op jit(solution)/shard_map/pallas_call | solution.py:183
  8.5 3.0 %collective-permute-start.16 = (f32[1,32]{1,0:T(1,128)S(1)}, f32[1,32]{1,0:T(1,128)S(1)}, u32[]{:S(2)}, u32[]{:S(2)}) collective-permute-start(f32[1,32]{1,0:T(1,128)S(1)} %reshape.1712), channel_id=1, source_target_pairs={{0,16},{16,0},{1,17},{17,1},{2,18},{18,2},{3,19},{19,3},{4,20},{20... | collective-permute-start | bytes 392 | tf_op jit(solution)/shard_map/ppermute | solution.py:19
  13.6 1.6 collective-permute-start.10
  16.0 2.2 %collective-permute-start.11 = (f32[8,64,128]{2,1,0:T(8,128)}, f32[8,64,128]{2,1,0:T(8,128)}, u32[]{:S(2)}, u32[]{:S(2)}) collective-permute-start(f32[8,64,128]{2,1,0:T(8,128)} %reshape.1710), channel_id=1, source_target_pairs={{0,3},{1,0},{2,1},{3,2},{4,7},{5,4},{6,5},{7,6},{8,11},{9,8},{10,9... | collective-permute-start | bytes 786440 | tf_op jit(solution)/shard_map/ppermute | solution.py:19
  20.1 1.7 fusion.109
  21.8 8.1 %fusion.108 = (f32[32,256,8]{2,1,0:T(8,128)}, f32[32,256,8]{2,1,0:T(8,128)}) fusion(f32[32,256,128]{2,1,0:T(8,128)} %c_ref.3), kind=kLoop, calls=%fused_computation.273 | loop fusion | bytes 1048576 | tf_op jit(solution)/shard_map/slice | solution.py:289
  36.2 1.6 collective-permute-start.18
  40.5 2.4 %collective-permute-start.21 = (f32[8,32]{1,0:T(8,128)S(1)}, f32[8,32]{1,0:T(8,128)S(1)}, u32[]{:S(2)}, u32[]{:S(2)}) collective-permute-start(f32[8,32]{1,0:T(8,128)S(1)} %bitcast.63), channel_id=1, source_target_pairs={{0,2},{1,3},{2,0},{3,1},{4,6},{5,7},{6,4},{7,5},{8,10},{9,11},{10,... | collective-permute-start | bytes 3080 | tf_op jit(solution)/shard_map/ppermute | solution.py:19
  42.8 1.5 collective-permute-start.22
  48.6 3.5 %copy.62 = f32[32,256,8]{1,2,0:T(8,128)} copy(f32[32,256,8]{2,1,0:T(8,128)} %get-tuple-element.81) | data formatting | bytes 524288
  52.1 2.8 %copy.65 = f32[32,256,8]{1,2,0:T(8,128)S(1)} copy(f32[32,256,8]{2,1,0:T(8,128)} %get-tuple-element.82) | data formatting | bytes 524288
  54.9 2.6 %copy.55 = f32[8,256,128]{1,2,0:T(8,128)} copy(f32[8,256,128]{2,1,0:T(8,128)} %get-tuple-element.86) | data formatting | bytes 2097152
  58.8 1.7 collective-permute-start.7
  61.2 1.8 fusion.38
  63.5 3.3 %collective-permute-start.1 = (f32[8,256,128]{1,2,0:T(8,128)}, f32[8,256,128]{1,2,0:T(8,128)}, u32[]{:S(2)}, u32[]{:S(2)}) collective-permute-start(f32[8,256,128]{1,2,0:T(8,128)} %copy.56), channel_id=1, source_target_pairs={{0,3},{1,0},{2,1},{3,2},{4,7},{5,4},{6,5},{7,6},{8,11},{9,8},{10,9... | collective-permute-start | bytes 3145736 | tf_op jit(solution)/shard_map/ppermute | solution.py:19
  69.4 1.6 copy.63
  71.0 2.0 maximum_bitcast_fusion
  73.6 1.6 copy.64
  75.2 1.7 copy.66
  76.9 1.9 reshape.1709
  78.8 1.9 reshape.1711
  81.7 1.7 collective-permute-start.13
  84.4 1.9 collective-permute-done.12
  86.3 1.4 collective-permute-start.9
  88.5 2.9 %slice_bitcast_fusion.1 = (f32[32,8,144]{1,2,0:T(8,128)}, f32[32,8,144]{1,2,0:T(8,128)}) fusion(f32[32,144,64]{2,1,0:T(8,128)S(1)} %pad_maximum_fusion), kind=kLoop, calls=%fused_computation.1 | loop fusion | bytes 589824 | tf_op jit(solution)/shard_map/transpose | solution.py:242
  91.5 2.8 %copy.47 = f32[32,8,144]{2,1,0:T(8,128)S(1)} copy(f32[32,8,144]{1,2,0:T(8,128)} %get-tuple-element.87) | data formatting | bytes 294912 | tf_op jit(solution)/shard_map/transpose | solution.py:242
  94.9 3.5 %copy.49 = f32[32,8,144]{2,1,0:T(8,128)} copy(f32[32,8,144]{1,2,0:T(8,128)} %get-tuple-element.88) | data formatting | bytes 294912 | tf_op jit(solution)/shard_map/transpose | solution.py:243
  98.3 1.4 collective-permute-start.15
  101.0 2.2 %copy-done.1 = f32[32,256,128]{2,1,0:T(8,128)S(1)} copy-done((f32[32,256,128]{2,1,0:T(8,128)S(1)}, f32[32,256,128]{2,1,0:T(8,128)}, u32[]{:S(2)}) %copy-start.1) | copy-done | bytes 4194328
  103.1 27.8 %shard_map.38.g_ref = f32[2,32,256,128]{3,2,1,0:T(8,128)S(1)} custom-call(f32[32,256,128]{2,1,0:T(8,128)S(1)} %copy-done.1, f32[32,8,128]{2,1,0:T(8,128)S(1)} %collective-permute-done.6.ylo_ref, f32[32,8,128]{2,1,0:T(8,128)S(1)} %collective-permute-done.7.yhi_ref, f32[32,16,272]{2,1,0:T(8,128)S(1)} %pad_maximum_fusion.2.xs_ref, ...), custom_call_target="tpu_custom_call" | custom-call | flops 3840000000 | bytes 12582912 | tf_op jit(solution)/shard_map/pallas_call | solution.py:75
  131.0 3.2 %copy-done.2 = f32[2,32,256,128]{3,2,1,0:T(8,128)} copy-done((f32[2,32,256,128]{3,2,1,0:T(8,128)}, f32[2,32,256,128]{3,2,1,0:T(8,128)S(1)}, u32[]{:S(2)}) %copy-start.2) | copy-done | bytes 8388632
  134.2 3.2 %copy.48 = f32[32,8,144]{1,2,0:T(8,128)} copy(f32[32,8,144]{2,1,0:T(8,128)} %collective-permute-done.14) | data formatting | bytes 294912 | tf_op jit(solution)/shard_map/ppermute | solution.py:19
  137.4 3.1 %copy.50 = f32[32,8,144]{1,2,0:T(8,128)} copy(f32[32,8,144]{2,1,0:T(8,128)} %collective-permute-done.15) | data formatting | bytes 294912 | tf_op jit(solution)/shard_map/ppermute | solution.py:19
  140.4 4.0 %pad_maximum_fusion.1.ext_ref = f32[32,144,80]{2,1,0:T(8,128)S(1)} fusion(f32[32,144,8]{2,1,0:T(8,128)} %bitcast.60, f32[32,8,64]{2,1,0:T(8,128)S(1)} %copy-done.11, f32[8,128,64]{2,1,0:T(8,128)} %reshape.1711, f32[16,128,64]{2,1,0:T(8,128)S(1)} %copy-done.6, f32[8,128,64]{2,1,0:T(8,128)} %reshape.1709, f32[32,8,64]{2,1,0:T(8,128)S(1)} %collective-permute-done.12, ...), kind=kLoop, calls=%fused_computation.3 | loop fusion | flops 2211840 | bytes 2949120 | tf_op jit(solution)/shard_map/concatenate | solution.py:244
  144.4 11.8 %shard_map.40.e_ref = f32[16,256,128]{2,1,0:T(8,128)S(1)} custom-call(f32[2,17]{1,0:T(2,128)S(1)} %get-tuple-element.110.w_ref, f32[32,144,80]{2,1,0:T(8,128)S(1)} %pad_maximum_fusion.1.ext_ref, f32[1,256,128]{2,1,0:T(8,128)S(1)} %convolution_bitcast_fusion.top_ref, bf16[2,80,128]{2,1,0:T(8,128)(2,1)S(1)} %reduce-precision_convert_fusion.3.bxh, ...), custom_call_target="tpu_custom_call" | custom-call | flops 10000000000 | bytes 10000000 | tf_op jit(solution)/shard_map/pallas_call | solution.py:217
  156.3 2.1 constant_dynamic-update-slice_fusion.1
  159.7 1.9 fusion.112
  161.6 1.7 copy.34
  164.3 2.1 copy.35
  166.5 1.7 collective-permute-start.3
  171.1 1.5 copy.58
  172.7 1.7 maximum_bitcast_fusion.2
  177.6 1.4 collective-permute-start.5
  179.0 3.4 %copy-done.3 = f32[2,32,256,128]{3,2,1,0:T(8,128)S(1)} copy-done((f32[2,32,256,128]{3,2,1,0:T(8,128)S(1)}, f32[2,32,256,128]{3,2,1,0:T(8,128)}, u32[]{:S(2)}) %copy-start.3) | copy-done | bytes 8388632
  182.4 11.9 %shard_map.41.p_ref = f32[32,256,128]{2,1,0:T(8,128)} custom-call(f32[2,17]{1,0:T(2,128)S(1)} %get-tuple-element.113.w_ref, f32[2,32,256,128]{3,2,1,0:T(8,128)S(1)} %copy-done.3, f32[16,256,128]{2,1,0:T(8,128)S(1)} %copy-done.5), custom_call_target="tpu_custom_call" | custom-call | flops 10000000000 | bytes 10485760 | tf_op jit(solution)/shard_map/pallas_call | solution.py:107
  194.3 1.9 copy.40.c_ref
  197.2 13.9 %shard_map.37.g_ref = f32[2,16,256,128]{3,2,1,0:T(8,128)S(1)} custom-call(f32[16,256,128]{2,1,0:T(8,128)S(1)} %copy.40.c_ref, f32[16,8,128]{2,1,0:T(8,128)S(1)} %collective-permute-done.2.ylo_ref, f32[16,8,128]{2,1,0:T(8,128)S(1)} %collective-permute-done.3.yhi_ref, f32[16,16,272]{2,1,0:T(8,128)S(1)} %pad_maximum_fusion.3.xs_ref, ...), custom_call_target="tpu_custom_call" | custom-call | flops 1920000000 | bytes 6291456 | tf_op jit(solution)/shard_map/pallas_call | solution.py:75
  211.2 4.9 %shard_map.42 = f32[32,256,128]{2,1,0:T(8,128)} custom-call(f32[2,17]{1,0:T(2,128)S(1)} %get-tuple-element.113.w_ref, f32[2,16,256,128]{3,2,1,0:T(8,128)S(1)} %shard_map.37.g_ref, f32[32,256,128]{2,1,0:T(8,128)} %shard_map.41.p_ref), custom_call_target="tpu_custom_call", output_to_operand_aliasing={{}: (2, {})} | custom-call | tf_op jit(solution)/shard_map/pallas_call | solution.py:154
  (152 shorter events, 40.9 us)
Async XLA Ops:
  8.5 27.6 %collective-permute-start.16 = (f32[1,32]{1,0:T(1,128)S(1)}, f32[1,32]{1,0:T(1,128)S(1)}, u32[]{:S(2)}, u32[]{:S(2)}) collective-permute-start(f32[1,32]{1,0:T(1,128)S(1)} %reshape.1712), channel_id=1, source_target_pairs={{0,16},{16,0},{1,17},{17,1},{2,18},{18,2},{3,19},{19,3},{4,20},{20... | collective-permute-start | bytes 392 | tf_op jit(solution)/shard_map/ppermute | solution.py:19
  13.6 63.3 %collective-permute-start.10 = (f32[8,64,128]{2,1,0:T(8,128)}, f32[8,64,128]{2,1,0:T(8,128)}, u32[]{:S(2)}, u32[]{:S(2)}) collective-permute-start(f32[8,64,128]{2,1,0:T(8,128)} %reshape.1708), channel_id=1, source_target_pairs={{0,1},{1,2},{2,3},{3,0},{4,5},{5,6},{6,7},{7,4},{8,9},{9,10},{10,1... | collective-permute-start | bytes 786440 | tf_op jit(solution)/shard_map/ppermute | solution.py:19
  16.0 62.8 %collective-permute-start.11 = (f32[8,64,128]{2,1,0:T(8,128)}, f32[8,64,128]{2,1,0:T(8,128)}, u32[]{:S(2)}, u32[]{:S(2)}) collective-permute-start(f32[8,64,128]{2,1,0:T(8,128)} %reshape.1710), channel_id=1, source_target_pairs={{0,3},{1,0},{2,1},{3,2},{4,7},{5,4},{6,5},{7,6},{8,11},{9,8},{10,9... | collective-permute-start | bytes 786440 | tf_op jit(solution)/shard_map/ppermute | solution.py:19
  21.8 8.1 %copy-start = (f32[32,256,128]{2,1,0:T(8,128)S(1)}, f32[32,256,128]{2,1,0:T(8,128)}, u32[]{:S(2)}) copy-start(f32[32,256,128]{2,1,0:T(8,128)} %c_ref.3) | copy-start | bytes 12582916
  29.9 1.2 copy-start.14
  31.1 2.2 %copy-start.15 = (f32[2,3,17]{2,0,1:T(2,128)S(1)}, f32[2,3,17]{2,0,1:T(2,128)}, u32[]{:S(2)}) copy-start(f32[2,3,17]{2,0,1:T(2,128)} %param.4) | copy-start | bytes 1228
  36.1 3.0 %collective-permute-start.17 = (f32[2,32]{1,0:T(2,128)S(1)}, f32[2,32]{1,0:T(2,128)S(1)}, u32[]{:S(2)}, u32[]{:S(2)}) collective-permute-start(f32[2,32]{1,0:T(2,128)S(1)} %bitcast.66), channel_id=1, source_target_pairs={{0,4},{4,8},{8,12},{12,0},{1,5},{5,9},{9,13},{13,1},{2,6},{6,10},{... | collective-permute-start | bytes 776 | tf_op jit(solution)/shard_map/ppermute | solution.py:19
  36.2 3.6 %collective-permute-start.18 = (f32[2,32]{1,0:T(2,128)S(1)}, f32[2,32]{1,0:T(2,128)S(1)}, u32[]{:S(2)}, u32[]{:S(2)}) collective-permute-start(f32[2,32]{1,0:T(2,128)S(1)} %bitcast.67), channel_id=1, source_target_pairs={{0,8},{4,12},{8,0},{12,4},{1,9},{5,13},{9,1},{13,5},{2,10},{6,14},... | collective-permute-start | bytes 776 | tf_op jit(solution)/shard_map/ppermute | solution.py:19
  37.8 2.7 %collective-permute-start.19 = (f32[2,32]{1,0:T(2,128)S(1)}, f32[2,32]{1,0:T(2,128)S(1)}, u32[]{:S(2)}, u32[]{:S(2)}) collective-permute-start(f32[2,32]{1,0:T(2,128)S(1)} %bitcast.68), channel_id=1, source_target_pairs={{0,12},{4,0},{8,4},{12,8},{1,13},{5,1},{9,5},{13,9},{2,14},{6,2},{... | collective-permute-start | bytes 776 | tf_op jit(solution)/shard_map/ppermute | solution.py:19
  40.5 18.3 %collective-permute-start.20 = (f32[8,32]{1,0:T(8,128)S(1)}, f32[8,32]{1,0:T(8,128)S(1)}, u32[]{:S(2)}, u32[]{:S(2)}) collective-permute-start(f32[8,32]{1,0:T(8,128)S(1)} %bitcast.62), channel_id=1, source_target_pairs={{0,1},{1,2},{2,3},{3,0},{4,5},{5,6},{6,7},{7,4},{8,9},{9,10},{10,1... | collective-permute-start | bytes 3080 | tf_op jit(solution)/shard_map/ppermute | solution.py:19
  40.5 18.3 %collective-permute-start.21 = (f32[8,32]{1,0:T(8,128)S(1)}, f32[8,32]{1,0:T(8,128)S(1)}, u32[]{:S(2)}, u32[]{:S(2)}) collective-permute-start(f32[8,32]{1,0:T(8,128)S(1)} %bitcast.63), channel_id=1, source_target_pairs={{0,2},{1,3},{2,0},{3,1},{4,6},{5,7},{6,4},{7,5},{8,10},{9,11},{10,... | collective-permute-start | bytes 3080 | tf_op jit(solution)/shard_map/ppermute | solution.py:19
  42.8 17.7 %collective-permute-start.22 = (f32[8,32]{1,0:T(8,128)S(1)}, f32[8,32]{1,0:T(8,128)S(1)}, u32[]{:S(2)}, u32[]{:S(2)}) collective-permute-start(f32[8,32]{1,0:T(8,128)S(1)} %bitcast.64), channel_id=1, source_target_pairs={{0,3},{1,0},{2,1},{3,2},{4,7},{5,4},{6,5},{7,6},{8,11},{9,8},{10,9... | collective-permute-start | bytes 3080 | tf_op jit(solution)/shard_map/ppermute | solution.py:19
  58.8 4.8 %collective-permute-start.6 = (f32[32,8,128]{2,1,0:T(8,128)}, f32[32,8,128]{2,1,0:T(8,128)S(1)}, u32[]{:S(2)}, u32[]{:S(2)}) collective-permute-start(f32[32,8,128]{2,1,0:T(8,128)} %get-tuple-element.84), channel_id=1, source_target_pairs={{0,4},{4,8},{8,12},{12,0},{1,5},{5,9},{9,13},{13,1},{2,6},{6,10},{... | collective-permute-start | bytes 393224 | tf_op jit(solution)/shard_map/ppermute | solution.py:19
  58.8 9.8 %collective-permute-start.7 = (f32[32,8,128]{2,1,0:T(8,128)}, f32[32,8,128]{2,1,0:T(8,128)S(1)}, u32[]{:S(2)}, u32[]{:S(2)}) collective-permute-start(f32[32,8,128]{2,1,0:T(8,128)} %get-tuple-element.83), channel_id=1, source_target_pairs={{0,12},{4,0},{8,4},{12,8},{1,13},{5,1},{9,5},{13,9},{2,14},{6,2},{... | collective-permute-start | bytes 393224 | tf_op jit(solution)/shard_map/ppermute | solution.py:19
  60.5 95.7 %collective-permute-start = (f32[8,256,128]{1,2,0:T(8,128)}, f32[8,256,128]{1,2,0:T(8,128)}, u32[]{:S(2)}, u32[]{:S(2)}) collective-permute-start(f32[8,256,128]{1,2,0:T(8,128)} %copy.55), channel_id=1, source_target_pairs={{0,1},{1,2},{2,3},{3,0},{4,5},{5,6},{6,7},{7,4},{8,9},{9,10},{10,1... | collective-permute-start | bytes 3145736 | tf_op jit(solution)/shard_map/ppermute | solution.py:19
  63.2 17.5 %copy-start.6 = (f32[16,128,64]{2,1,0:T(8,128)S(1)}, f32[16,128,64]{2,1,0:T(8,128)}, u32[]{:S(2)}) copy-start(f32[16,128,64]{2,1,0:T(8,128)} %shard_map.39) | copy-start | bytes 1572868
  63.5 94.8 %collective-permute-start.1 = (f32[8,256,128]{1,2,0:T(8,128)}, f32[8,256,128]{1,2,0:T(8,128)}, u32[]{:S(2)}, u32[]{:S(2)}) collective-permute-start(f32[8,256,128]{1,2,0:T(8,128)} %copy.56), channel_id=1, source_target_pairs={{0,3},{1,0},{2,1},{3,2},{4,7},{5,4},{6,5},{7,6},{8,11},{9,8},{10,9... | collective-permute-start | bytes 3145736 | tf_op jit(solution)/shard_map/ppermute | solution.py:19
  73.0 25.4 %collective-permute-start.8 = (f32[32,8,272]{2,1,0:T(8,128)}, f32[32,8,272]{2,1,0:T(8,128)}, u32[]{:S(2)}, u32[]{:S(2)}) collective-permute-start(f32[32,8,272]{2,1,0:T(8,128)} %maximum_bitcast_fusion), channel_id=1, source_target_pairs={{0,16},{16,0},{1,17},{17,1},{2,18},{18,2},{3,19},{19,3},{4,20},{20... | collective-permute-start | bytes 835592 | tf_op jit(solution)/shard_map/ppermute | solution.py:19
  80.7 2.8 %copy-start.12 = (f32[32,8,8]{1,2,0:T(8,128)S(1)}, f32[32,8,8]{1,2,0:T(8,128)}, u32[]{:S(2)}) copy-start(f32[32,8,8]{1,2,0:T(8,128)} %copy.64) | copy-start | bytes 24580
  80.7 2.8 %copy-start.13 = (f32[32,8,8]{1,2,0:T(8,128)S(1)}, f32[32,8,8]{1,2,0:T(8,128)}, u32[]{:S(2)}) copy-start(f32[32,8,8]{1,2,0:T(8,128)} %copy.66) | copy-start | bytes 24580
  80.7 7.6 %copy-start.8 = (f32[8,128,64]{2,1,0:T(8,128)S(1)}, f32[8,128,64]{2,1,0:T(8,128)}, u32[]{:S(2)}) copy-start(f32[8,128,64]{2,1,0:T(8,128)} %reshape.1709) | copy-start | bytes 786436
  80.7 7.6 %copy-start.9 = (f32[8,128,64]{2,1,0:T(8,128)S(1)}, f32[8,128,64]{2,1,0:T(8,128)}, u32[]{:S(2)}) copy-start(f32[8,128,64]{2,1,0:T(8,128)} %reshape.1711) | copy-start | bytes 786436
  81.7 4.6 %collective-permute-start.12 = (f32[32,8,64]{2,1,0:T(8,128)S(1)}, f32[32,8,64]{2,1,0:T(8,128)S(1)}, u32[]{:S(2)}, u32[]{:S(2)}) collective-permute-start(f32[32,8,64]{2,1,0:T(8,128)S(1)} %get-tuple-element.89), channel_id=1, source_target_pairs={{0,4},{4,8},{8,12},{12,0},{1,5},{5,9},{9,13},{13,1},{2,6},{6,10},{... | collective-permute-start | bytes 196616 | tf_op jit(solution)/shard_map/ppermute | solution.py:19
  81.7 6.0 %collective-permute-start.13 = (f32[32,8,64]{2,1,0:T(8,128)S(1)}, f32[32,8,64]{2,1,0:T(8,128)S(1)}, u32[]{:S(2)}, u32[]{:S(2)}) collective-permute-start(f32[32,8,64]{2,1,0:T(8,128)S(1)} %get-tuple-element.90), channel_id=1, source_target_pairs={{0,12},{4,0},{8,4},{12,8},{1,13},{5,1},{9,5},{13,9},{2,14},{6,2},{... | collective-permute-start | bytes 196616 | tf_op jit(solution)/shard_map/ppermute | solution.py:19
  86.3 13.5 %collective-permute-start.9 = (f32[32,8,272]{2,1,0:T(8,128)}, f32[32,8,272]{2,1,0:T(8,128)}, u32[]{:S(2)}, u32[]{:S(2)}) collective-permute-start(f32[32,8,272]{2,1,0:T(8,128)} %maximum_bitcast_fusion.1), channel_id=1, source_target_pairs={{0,16},{16,0},{1,17},{17,1},{2,18},{18,2},{3,19},{19,3},{4,20},{20... | collective-permute-start | bytes 835592 | tf_op jit(solution)/shard_map/ppermute | solution.py:19
  87.7 0.6 copy-start.10
  94.2 40.0 %collective-permute-start.14 = (f32[32,8,144]{2,1,0:T(8,128)S(1)}, f32[32,8,144]{2,1,0:T(8,128)}, u32[]{:S(2)}, u32[]{:S(2)}) collective-permute-start(f32[32,8,144]{2,1,0:T(8,128)S(1)} %copy.47), channel_id=1, source_target_pairs={{0,16},{16,0},{1,17},{17,1},{2,18},{18,2},{3,19},{19,3},{4,20},{20... | collective-permute-start | bytes 442376 | tf_op jit(solution)/shard_map/ppermute | solution.py:19
  98.3 39.0 %collective-permute-start.15 = (f32[32,8,144]{2,1,0:T(8,128)}, f32[32,8,144]{2,1,0:T(8,128)}, u32[]{:S(2)}, u32[]{:S(2)}) collective-permute-start(f32[32,8,144]{2,1,0:T(8,128)} %copy.49), channel_id=1, source_target_pairs={{0,16},{16,0},{1,17},{17,1},{2,18},{18,2},{3,19},{19,3},{4,20},{20... | collective-permute-start | bytes 442376 | tf_op jit(solution)/shard_map/ppermute | solution.py:19
  100.9 2.2 %copy-start.1 = (f32[32,256,128]{2,1,0:T(8,128)S(1)}, f32[32,256,128]{2,1,0:T(8,128)}, u32[]{:S(2)}) copy-start(f32[32,256,128]{2,1,0:T(8,128)} %c_ref.3) | copy-start | bytes 12582916
  130.9 3.2 %copy-start.2 = (f32[2,32,256,128]{3,2,1,0:T(8,128)}, f32[2,32,256,128]{3,2,1,0:T(8,128)S(1)}, u32[]{:S(2)}) copy-start(f32[2,32,256,128]{3,2,1,0:T(8,128)S(1)} %shard_map.38.g_ref) | copy-start | bytes 25165828
  134.2 6.3 %copy-start.11 = (f32[32,8,64]{2,1,0:T(8,128)S(1)}, f32[32,8,64]{2,1,0:T(8,128)}, u32[]{:S(2)}) copy-start(f32[32,8,64]{2,1,0:T(8,128)} %copy-done.10) | copy-start | bytes 196612
  156.2 5.3 %copy-start.4 = (f32[16,256,128]{2,1,0:T(8,128)}, f32[16,256,128]{2,1,0:T(8,128)S(1)}, u32[]{:S(2)}) copy-start(f32[16,256,128]{2,1,0:T(8,128)S(1)} %shard_map.40.e_ref) | copy-start | bytes 6291460
  159.6 2.0 copy-start.7
  161.6 17.4 %copy-start.5 = (f32[16,256,128]{2,1,0:T(8,128)S(1)}, f32[16,256,128]{2,1,0:T(8,128)}, u32[]{:S(2)}) copy-start(f32[16,256,128]{2,1,0:T(8,128)} %copy-done.4) | copy-start | bytes 6291460
  163.3 4.9 %collective-permute-start.2 = (f32[16,8,128]{2,1,0:T(8,128)S(1)}, f32[16,8,128]{2,1,0:T(8,128)S(1)}, u32[]{:S(2)}, u32[]{:S(2)}) collective-permute-start(f32[16,8,128]{2,1,0:T(8,128)S(1)} %copy.34), channel_id=1, source_target_pairs={{0,4},{4,8},{8,12},{12,0},{1,5},{5,9},{9,13},{13,1},{2,6},{6,10},{... | collective-permute-start | bytes 196616 | tf_op jit(solution)/shard_map/ppermute | solution.py:19
  166.5 4.0 %collective-permute-start.3 = (f32[16,8,128]{2,1,0:T(8,128)}, f32[16,8,128]{2,1,0:T(8,128)S(1)}, u32[]{:S(2)}, u32[]{:S(2)}) collective-permute-start(f32[16,8,128]{2,1,0:T(8,128)} %copy.35), channel_id=1, source_target_pairs={{0,12},{4,0},{8,4},{12,8},{1,13},{5,1},{9,5},{13,9},{2,14},{6,2},{... | collective-permute-start | bytes 196616 | tf_op jit(solution)/shard_map/ppermute | solution.py:19
  174.3 21.9 %collective-permute-start.4 = (f32[16,8,272]{2,1,0:T(8,128)}, f32[16,8,272]{2,1,0:T(8,128)}, u32[]{:S(2)}, u32[]{:S(2)}) collective-permute-start(f32[16,8,272]{2,1,0:T(8,128)} %maximum_bitcast_fusion.2), channel_id=1, source_target_pairs={{0,16},{16,0},{1,17},{17,1},{2,18},{18,2},{3,19},{19,3},{4,20},{20... | collective-permute-start | bytes 417800 | tf_op jit(solution)/shard_map/ppermute | solution.py:19
  177.6 18.7 %collective-permute-start.5 = (f32[16,8,272]{2,1,0:T(8,128)}, f32[16,8,272]{2,1,0:T(8,128)S(1)}, u32[]{:S(2)}, u32[]{:S(2)}) collective-permute-start(f32[16,8,272]{2,1,0:T(8,128)} %maximum_bitcast_fusion.3), channel_id=1, source_target_pairs={{0,16},{16,0},{1,17},{17,1},{2,18},{18,2},{3,19},{19,3},{4,20},{20... | collective-permute-start | bytes 417800 | tf_op jit(solution)/shard_map/ppermute | solution.py:19
  179.0 3.4 %copy-start.3 = (f32[2,32,256,128]{3,2,1,0:T(8,128)S(1)}, f32[2,32,256,128]{3,2,1,0:T(8,128)}, u32[]{:S(2)}) copy-start(f32[2,32,256,128]{3,2,1,0:T(8,128)} %copy-done.2) | copy-start | bytes 25165828
where the time goes:
time: 217 us; the launch traced here: 216 us
  local copies, waits for them, and re-layouts  84.5 us (39%)
  Pallas kernels  75.6 us (35%)
  starting transfers between devices  28.9 us (13%)
  other arithmetic  19.9 us (9%)
  waiting for transfers between devices  3.81 us (2%)
  matrix products  2.83 us (1%)
    pallas_call x2, Pallas kernels, xy_pass(): pl.pallas_call(functools.partial(xy_kernel, planes, size_y, size_x), grid...  41.7 us
    unnamed x45, local copies, waits for them, and re-layouts  31.9 us
    ppermute x23, starting transfers between devices, shift(): return lax.ppermute(block, axis, [(i, (i + by) % n) for i in range(n)])  28.9 us
    pallas_call x1, Pallas kernels, z_own(): pl.pallas_call(functools.partial(z_own_kernel, size_z, blk // 8), grid=(s...  11.9 us
    pallas_call x1, Pallas kernels, coarse_level(): pl.pallas_call(functools.partial(coarse_kernel, planes), grid=(size_z //...  11.8 us
    slice x2, local copies, waits for them, and re-layouts, turned(): block[:, :, cols]  9.13 us
    ppermute x2, local copies, waits for them, and re-layouts, shift(): return lax.ppermute(block, axis, [(i, (i + by) % n) for i in range(n)])  6.26 us
    slice x3, local copies, waits for them, and re-layouts, sides(): yhi = shift(block[:, :r], 'gy', -1)  5.71 us
  transfers between devices with their start and end apart: 23, of which 4 were waited for; matrix products, arithmetic and copies ran while one was open for 39% of the time, Pallas kernels for 24%

commit v1 on v0

--- a/solution.py
+++ b/solution.py
@@ -62,9 +62,12 @@
         parts.append(mid[p * ext_y:(p + 1) * ext_y] + edge)
     for t in range(2):
         right = jnp.concatenate([part[:, t * size_x:(t + 1) * size_x] for part in parts], axis=1)
-        out = mm3((byh[t], byl[t]), split_in(right))
-        for p in range(planes):
-            g_ref[t, p] = out[:, p * size_x:(p + 1) * size_x]
+        high, low = split_in(right)
+        chunk, reach = byh.shape[1:]
+        for y in range(0, size_y, chunk):
+            out = mm3((byh[t], byl[t]), (high[y:y + reach], low[y:y + reach]))
+            for p in range(planes):
+                g_ref[t, p, y:y + chunk, :] = out[:, p * size_x:(p + 1) * size_x]
 
 
 def xy_pass(block, ylo, yhi, xs, mats):
@@ -303,7 +306,8 @@
     band_x = band(fine_taps[:, 0], size_x + 2 * r, size_x)
     band_x = jnp.concatenate([band_x[0], band_x[1]], axis=1)
     edge_x = jnp.concatenate([band_x[:r], band_x[-r:]], axis=0)
-    band_y = band(fine_taps[:, 1], size_y + 2 * r, size_y).transpose(0, 2, 1)
+    chunk = 128 if size_y % 128 == 0 else size_y
+    band_y = band(fine_taps[:, 1], chunk + 2 * r, chunk).transpose(0, 2, 1)
     mats = split(band_x[r:-r]) + split(edge_x) + split(band_y)
     taps_z = fine_taps[:, 2]
 

time: 217 us -> 189 us (0.87)
  Pallas kernels: 75.6 us -> 62 us
  local copies, waits for them, and re-layouts: 84.5 us -> 71 us
  other arithmetic: 19.9 us -> 16.8 us
    pallas_call x2, Pallas kernels: 41.7 us -> 28.1 us  [xy_pass(): pl.pallas_call(functools.partial(xy_kernel, planes, size_y, size_x), grid...]
    unnamed x45 -> x51, local copies, waits for them, and re-layouts: 31.9 us -> 23 us
    transpose x4, other arithmetic: 5.39 us -> 2.21 us  [turned(): return strip.transpose(0, 2, 1)]
  transfers between devices with their start and end apart: 23 -> 23, of which waited for: 4 -> 4; matrix products, arithmetic and copies ran while one was open for 39% -> 38% of each run, Pallas kernels for 24% -> 23%
where the time goes in v1:
time: 189 us; the launch traced here: 188 us
  local copies, waits for them, and re-layouts  71 us (38%)
  Pallas kernels  62 us (33%)
  starting transfers between devices  29.2 us (15%)
  other arithmetic  16.8 us (9%)
  waiting for transfers between devices  4.45 us (2%)
  matrix products  3.54 us (2%)
    ppermute x23, starting transfers between devices, shift(): return lax.ppermute(block, axis, [(i, (i + by) % n) for i in range(n)])  29.2 us
    pallas_call x2, Pallas kernels, xy_pass(): pl.pallas_call(functools.partial(xy_kernel, planes, size_y, size_x), grid...  28.1 us
    unnamed x51, local copies, waits for them, and re-layouts  23 us
    pallas_call x1, Pallas kernels, z_own(): pl.pallas_call(functools.partial(z_own_kernel, size_z, blk // 8), grid=(s...  12 us
    pallas_call x1, Pallas kernels, coarse_level(): pl.pallas_call(functools.partial(coarse_kernel, planes), grid=(size_z //...  11.8 us
    slice x2, local copies, waits for them, and re-layouts, turned(): block[:, :, cols]  9.13 us
    transpose x2, local copies, waits for them, and re-layouts, coarse_halo(): low = shift(ext[:, :, -r:].transpose(0, 2, 1), 'gx', 1).transpose(0, 2, 1)  6.41 us
    ppermute x2, local copies, waits for them, and re-layouts, shift(): return lax.ppermute(block, axis, [(i, (i + by) % n) for i in range(n)])  6.27 us
  transfers between devices with their start and end apart: 23, of which 4 were waited for; matrix products, arithmetic and copies ran while one was open for 38% of the time, Pallas kernels for 23%

profile of v1, /device:TPU:0, one launch (start us, length us, event | category | flops | bytes accessed | tf_op | source)
XLA Modules:
  0.0 187.6 jit_solution(5336924275962150883)
XLA Ops:
  1.3 5.2 %shard_map.39 = f32[16,128,64]{2,1,0:T(8,128)} custom-call(f32[32,256,128]{2,1,0:T(8,128)} %c_ref.3, bf16[128,256]{1,0:T(8,128)(2,1)} %select_convert_fusion.py_ref, bf16[128,64]{1,0:T(8,128)(2,1)} %select_convert_fusion.1.px_ref), custom_call_target="tpu_custom_call" | custom-call | tf_op jit(solution)/shard_map/pallas_call | solution.py:186
  6.5 1.3 reduce_sum.9
  8.5 3.0 %collective-permute-start.16 = (f32[1,32]{1,0:T(1,128)S(1)}, f32[1,32]{1,0:T(1,128)}, u32[]{:S(2)}, u32[]{:S(2)}) collective-permute-start(f32[1,32]{1,0:T(1,128)S(1)} %reshape.1472), channel_id=1, source_target_pairs={{0,16},{16,0},{1,17},{17,1},{2,18},{18,2},{3,19},{19,3},{4,20},{20... | collective-permute-start | bytes 392 | tf_op jit(solution)/shard_map/ppermute | solution.py:19
  11.5 1.3 fusion.113
  13.6 1.6 collective-permute-start.10
  16.0 2.2 %collective-permute-start.11 = (f32[8,64,128]{2,1,0:T(8,128)}, f32[8,64,128]{2,1,0:T(8,128)}, u32[]{:S(2)}, u32[]{:S(2)}) collective-permute-start(f32[8,64,128]{2,1,0:T(8,128)} %reshape.1470), channel_id=1, source_target_pairs={{0,3},{1,0},{2,1},{3,2},{4,7},{5,4},{6,5},{7,6},{8,11},{9,8},{10,9... | collective-permute-start | bytes 786440 | tf_op jit(solution)/shard_map/ppermute | solution.py:19
  19.7 1.6 fusion.109
  21.3 8.1 %fusion.108 = (f32[32,256,8]{2,1,0:T(8,128)}, f32[32,256,8]{2,1,0:T(8,128)}) fusion(f32[32,256,128]{2,1,0:T(8,128)} %c_ref.3), kind=kLoop, calls=%fused_computation.273 | loop fusion | bytes 1048576 | tf_op jit(solution)/shard_map/slice | solution.py:292
  35.1 1.6 collective-permute-start.18
  36.7 1.4 collective-permute-start.19
  39.4 2.4 %collective-permute-start.21 = (f32[8,32]{1,0:T(8,128)S(1)}, f32[8,32]{1,0:T(8,128)}, u32[]{:S(2)}, u32[]{:S(2)}) collective-permute-start(f32[8,32]{1,0:T(8,128)S(1)} %bitcast.63), channel_id=1, source_target_pairs={{0,2},{1,3},{2,0},{3,1},{4,6},{5,7},{6,4},{7,5},{8,10},{9,11},{10,... | collective-permute-start | bytes 3080 | tf_op jit(solution)/shard_map/ppermute | solution.py:19
  41.8 1.5 collective-permute-start.22
  44.7 1.2 copy.51
  46.8 1.9 %add.190 = f32[4,1024]{1,0:T(4,128)} reshape(f32[4,4,4,2,1,8,4]{6,5,3,2,1,0,4:T(8,128)} %add.189) | data formatting | bytes 32768 | tf_op jit(solution)/shard_map/add | solution.py:275
  48.7 2.8 %copy.62 = f32[32,256,8]{1,2,0:T(8,128)S(1)} copy(f32[32,256,8]{2,1,0:T(8,128)} %get-tuple-element.81) | data formatting | bytes 524288
  51.5 3.5 %copy.65 = f32[32,256,8]{1,2,0:T(8,128)} copy(f32[32,256,8]{2,1,0:T(8,128)} %get-tuple-element.82) | data formatting | bytes 524288
  55.0 1.3 copy.55
  56.3 1.3 copy.56
  57.6 1.7 collective-permute-start.7
  60.7 2.6 %fusion.38 = f32[1,8,4]{2,0,1:T(1,128)S(1)} fusion(f32[1024,1,1]{0,1,2:T(1,128)S(1)} %reshape.1475, f32[4,1024]{1,0:T(4,128)} %add.190, f32[8,1024]{1,0:T(8,128)S(1)} %copy.51), kind=kOutput, calls=%fused_computation.71 | convolution fusion | flops 491520 | bytes 53376 | tf_op jit(solution)/shard_map/dot_general | solution.py:281
  63.8 3.5 %collective-permute-start.1 = (f32[8,256,128]{1,2,0:T(8,128)}, f32[8,256,128]{1,2,0:T(8,128)}, u32[]{:S(2)}, u32[]{:S(2)}) collective-permute-start(f32[8,256,128]{1,2,0:T(8,128)} %copy.56), channel_id=1, source_target_pairs={{0,3},{1,0},{2,1},{3,2},{4,7},{5,4},{6,5},{7,6},{8,11},{9,8},{10,9... | collective-permute-start | bytes 3145736 | tf_op jit(solution)/shard_map/ppermute | solution.py:19
  73.0 1.7 collective-permute-start.13
  75.7 1.9 %collective-permute-done.12 = f32[32,8,64]{2,1,0:T(8,128)S(1)} collective-permute-done((f32[32,8,64]{2,1,0:T(8,128)S(1)}, f32[32,8,64]{2,1,0:T(8,128)S(1)}, u32[]{:S(2)}, u32[]{:S(2)}) %collective-permute-start.12) | collective-permute-done | bytes 65568 | tf_op jit(solution)/shard_map/ppermute | solution.py:19
  77.6 1.5 collective-permute-start.9
  80.0 2.9 %slice_bitcast_fusion.1 = (f32[32,8,144]{1,2,0:T(8,128)}, f32[32,8,144]{1,2,0:T(8,128)}) fusion(f32[32,144,64]{2,1,0:T(8,128)S(1)} %pad_maximum_fusion), kind=kLoop, calls=%fused_computation.1 | loop fusion | bytes 589824 | tf_op jit(solution)/shard_map/transpose | solution.py:245
  82.9 3.5 %copy.47 = f32[32,8,144]{2,1,0:T(8,128)} copy(f32[32,8,144]{1,2,0:T(8,128)} %get-tuple-element.87) | data formatting | bytes 294912 | tf_op jit(solution)/shard_map/transpose | solution.py:245
  87.0 3.5 %copy.49 = f32[32,8,144]{2,1,0:T(8,128)} copy(f32[32,8,144]{1,2,0:T(8,128)} %get-tuple-element.88) | data formatting | bytes 294912 | tf_op jit(solution)/shard_map/transpose | solution.py:246
  90.5 1.4 collective-permute-start.15
  93.1 2.2 %copy-done.1 = f32[32,256,128]{2,1,0:T(8,128)S(1)} copy-done((f32[32,256,128]{2,1,0:T(8,128)S(1)}, f32[32,256,128]{2,1,0:T(8,128)}, u32[]{:S(2)}) %copy-start.1) | copy-done | bytes 4194328
  95.2 18.7 %shard_map.38.g_ref = f32[2,32,256,128]{3,2,1,0:T(8,128)S(1)} custom-call(f32[32,256,128]{2,1,0:T(8,128)S(1)} %copy-done.1, f32[32,8,128]{2,1,0:T(8,128)S(1)} %collective-permute-done.6.ylo_ref, f32[32,8,128]{2,1,0:T(8,128)S(1)} %collective-permute-done.7.yhi_ref, f32[32,16,272]{2,1,0:T(8,128)S(1)} %pad_maximum_fusion.2.xs_ref, ...), custom_call_target="tpu_custom_call" | custom-call | flops 3840000000 | bytes 12582912 | tf_op jit(solution)/shard_map/pallas_call | solution.py:78
  114.0 3.2 %copy-done.2 = f32[2,32,256,128]{3,2,1,0:T(8,128)} copy-done((f32[2,32,256,128]{3,2,1,0:T(8,128)}, f32[2,32,256,128]{3,2,1,0:T(8,128)S(1)}, u32[]{:S(2)}) %copy-start.2) | copy-done | bytes 8388632
  117.2 3.2 %copy.48 = f32[32,8,144]{1,2,0:T(8,128)} copy(f32[32,8,144]{2,1,0:T(8,128)} %collective-permute-done.14) | data formatting | bytes 294912 | tf_op jit(solution)/shard_map/ppermute | solution.py:19
  120.4 3.1 %copy.50 = f32[32,8,144]{1,2,0:T(8,128)} copy(f32[32,8,144]{2,1,0:T(8,128)} %collective-permute-done.15) | data formatting | bytes 294912 | tf_op jit(solution)/shard_map/ppermute | solution.py:19
  123.5 3.7 %pad_maximum_fusion.1.ext_ref = f32[32,144,80]{2,1,0:T(8,128)S(1)} fusion(f32[32,144,8]{2,1,0:T(8,128)} %bitcast.60, f32[32,8,64]{2,1,0:T(8,128)S(1)} %copy-done.12, f32[8,128,64]{2,1,0:T(8,128)S(1)} %reshape.1471, f32[16,128,64]{2,1,0:T(8,128)S(1)} %copy-done.6, f32[8,128,64]{2,1,0:T(8,128)S(1)} %reshape.1469, f32[32,8,64]{2,1,0:T(8,128)S(1)} %copy-done.10, ...), kind=kLoop, calls=%fused_computation.3 | loop fusion | flops 2211840 | bytes 2949120 | tf_op jit(solution)/shard_map/concatenate | solution.py:247
  127.1 11.8 %shard_map.40.e_ref = f32[16,256,128]{2,1,0:T(8,128)S(1)} custom-call(f32[2,17]{1,0:T(2,128)S(1)} %get-tuple-element.110.w_ref, f32[32,144,80]{2,1,0:T(8,128)S(1)} %pad_maximum_fusion.1.ext_ref, f32[1,256,128]{2,1,0:T(8,128)S(1)} %convolution_bitcast_fusion.top_ref, bf16[2,80,128]{2,1,0:T(8,128)(2,1)S(1)} %reduce-precision_convert_fusion.3.bxh, ...), custom_call_target="tpu_custom_call" | custom-call | flops 10000000000 | bytes 10000000 | tf_op jit(solution)/shard_map/pallas_call | solution.py:220
  138.9 2.1 %constant_dynamic-update-slice_fusion.1 = f32[16,256,128]{1,2,0:T(8,128)S(1)} fusion(f32[8,256,128]{1,2,0:T(8,128)} %collective-permute-done), kind=kLoop, calls=%fused_computation.151 | loop fusion | bytes 2097152
  141.0 1.3 constant_dynamic-update-slice_fusion
  142.3 1.9 fusion.112
  144.3 1.7 copy.34
  147.0 1.5 copy.35
  148.5 1.8 collective-permute-start.3
  150.4 1.7 collective-permute-done.3.yhi_ref
  153.5 1.5 collective-permute-start.5
  154.9 3.4 %copy-done.3 = f32[2,32,256,128]{3,2,1,0:T(8,128)S(1)} copy-done((f32[2,32,256,128]{3,2,1,0:T(8,128)S(1)}, f32[2,32,256,128]{3,2,1,0:T(8,128)}, u32[]{:S(2)}) %copy-start.3) | copy-done | bytes 8388632
  158.3 12.0 %shard_map.41.p_ref = f32[32,256,128]{2,1,0:T(8,128)} custom-call(f32[2,17]{1,0:T(2,128)S(1)} %get-tuple-element.113.w_ref, f32[2,32,256,128]{3,2,1,0:T(8,128)S(1)} %copy-done.3, f32[16,256,128]{2,1,0:T(8,128)S(1)} %copy-done.5), custom_call_target="tpu_custom_call" | custom-call | flops 10000000000 | bytes 10485760 | tf_op jit(solution)/shard_map/pallas_call | solution.py:110
  170.4 1.9 %copy.40.c_ref = f32[16,256,128]{2,1,0:T(8,128)S(1)} copy(f32[16,256,128]{1,2,0:T(8,128)} %copy-done.7) | data formatting | bytes 4194304 | tf_op jit(solution)/shard_map/concatenate | solution.py:321
  173.4 9.4 %shard_map.37.g_ref = f32[2,16,256,128]{3,2,1,0:T(8,128)S(1)} custom-call(f32[16,256,128]{2,1,0:T(8,128)S(1)} %copy.40.c_ref, f32[16,8,128]{2,1,0:T(8,128)S(1)} %collective-permute-done.2.ylo_ref, f32[16,8,128]{2,1,0:T(8,128)S(1)} %collective-permute-done.3.yhi_ref, f32[16,16,272]{2,1,0:T(8,128)S(1)} %pad_maximum_fusion.3.xs_ref, ...), custom_call_target="tpu_custom_call" | custom-call | flops 1920000000 | bytes 6291456 | tf_op jit(solution)/shard_map/pallas_call | solution.py:78
  182.7 4.9 %shard_map.42 = f32[32,256,128]{2,1,0:T(8,128)} custom-call(f32[2,17]{1,0:T(2,128)S(1)} %get-tuple-element.113.w_ref, f32[2,16,256,128]{3,2,1,0:T(8,128)S(1)} %shard_map.37.g_ref, f32[32,256,128]{2,1,0:T(8,128)} %shard_map.41.p_ref), custom_call_target="tpu_custom_call", output_to_operand_aliasing={{}: (2, {})} | custom-call | tf_op jit(solution)/shard_map/pallas_call | solution.py:157
  (158 shorter events, 28.9 us)
Async XLA Ops:
  8.5 26.0 %collective-permute-start.16 = (f32[1,32]{1,0:T(1,128)S(1)}, f32[1,32]{1,0:T(1,128)}, u32[]{:S(2)}, u32[]{:S(2)}) collective-permute-start(f32[1,32]{1,0:T(1,128)S(1)} %reshape.1472), channel_id=1, source_target_pairs={{0,16},{16,0},{1,17},{17,1},{2,18},{18,2},{3,19},{19,3},{4,20},{20... | collective-permute-start | bytes 392 | tf_op jit(solution)/shard_map/ppermute | solution.py:19
  13.6 57.1 %collective-permute-start.10 = (f32[8,64,128]{2,1,0:T(8,128)}, f32[8,64,128]{2,1,0:T(8,128)}, u32[]{:S(2)}, u32[]{:S(2)}) collective-permute-start(f32[8,64,128]{2,1,0:T(8,128)} %reshape.1468), channel_id=1, source_target_pairs={{0,1},{1,2},{2,3},{3,0},{4,5},{5,6},{6,7},{7,4},{8,9},{9,10},{10,1... | collective-permute-start | bytes 786440 | tf_op jit(solution)/shard_map/ppermute | solution.py:19
  16.0 55.8 %collective-permute-start.11 = (f32[8,64,128]{2,1,0:T(8,128)}, f32[8,64,128]{2,1,0:T(8,128)}, u32[]{:S(2)}, u32[]{:S(2)}) collective-permute-start(f32[8,64,128]{2,1,0:T(8,128)} %reshape.1470), channel_id=1, source_target_pairs={{0,3},{1,0},{2,1},{3,2},{4,7},{5,4},{6,5},{7,6},{8,11},{9,8},{10,9... | collective-permute-start | bytes 786440 | tf_op jit(solution)/shard_map/ppermute | solution.py:19
  21.3 8.1 %copy-start = (f32[32,256,128]{2,1,0:T(8,128)S(1)}, f32[32,256,128]{2,1,0:T(8,128)}, u32[]{:S(2)}) copy-start(f32[32,256,128]{2,1,0:T(8,128)} %c_ref.3) | copy-start | bytes 12582916
  29.5 0.7 copy-start.15
  30.2 2.2 %copy-start.16 = (f32[2,3,17]{2,0,1:T(2,128)S(1)}, f32[2,3,17]{2,0,1:T(2,128)}, u32[]{:S(2)}) copy-start(f32[2,3,17]{2,0,1:T(2,128)} %param.4) | copy-start | bytes 1228
  35.1 3.5 %collective-permute-start.17 = (f32[2,32]{1,0:T(2,128)S(1)}, f32[2,32]{1,0:T(2,128)S(1)}, u32[]{:S(2)}, u32[]{:S(2)}) collective-permute-start(f32[2,32]{1,0:T(2,128)S(1)} %bitcast.66), channel_id=1, source_target_pairs={{0,4},{4,8},{8,12},{12,0},{1,5},{5,9},{9,13},{13,1},{2,6},{6,10},{... | collective-permute-start | bytes 776 | tf_op jit(solution)/shard_map/ppermute | solution.py:19
  35.1 3.6 %collective-permute-start.18 = (f32[2,32]{1,0:T(2,128)S(1)}, f32[2,32]{1,0:T(2,128)S(1)}, u32[]{:S(2)}, u32[]{:S(2)}) collective-permute-start(f32[2,32]{1,0:T(2,128)S(1)} %bitcast.67), channel_id=1, source_target_pairs={{0,8},{4,12},{8,0},{12,4},{1,9},{5,13},{9,1},{13,5},{2,10},{6,14},... | collective-permute-start | bytes 776 | tf_op jit(solution)/shard_map/ppermute | solution.py:19
  36.7 2.7 %collective-permute-start.19 = (f32[2,32]{1,0:T(2,128)S(1)}, f32[2,32]{1,0:T(2,128)S(1)}, u32[]{:S(2)}, u32[]{:S(2)}) collective-permute-start(f32[2,32]{1,0:T(2,128)S(1)} %bitcast.68), channel_id=1, source_target_pairs={{0,12},{4,0},{8,4},{12,8},{1,13},{5,1},{9,5},{13,9},{2,14},{6,2},{... | collective-permute-start | bytes 776 | tf_op jit(solution)/shard_map/ppermute | solution.py:19
  39.4 18.2 %collective-permute-start.20 = (f32[8,32]{1,0:T(8,128)S(1)}, f32[8,32]{1,0:T(8,128)}, u32[]{:S(2)}, u32[]{:S(2)}) collective-permute-start(f32[8,32]{1,0:T(8,128)S(1)} %bitcast.62), channel_id=1, source_target_pairs={{0,1},{1,2},{2,3},{3,0},{4,5},{5,6},{6,7},{7,4},{8,9},{9,10},{10,1... | collective-permute-start | bytes 3080 | tf_op jit(solution)/shard_map/ppermute | solution.py:19
  39.4 18.2 %collective-permute-start.21 = (f32[8,32]{1,0:T(8,128)S(1)}, f32[8,32]{1,0:T(8,128)}, u32[]{:S(2)}, u32[]{:S(2)}) collective-permute-start(f32[8,32]{1,0:T(8,128)S(1)} %bitcast.63), channel_id=1, source_target_pairs={{0,2},{1,3},{2,0},{3,1},{4,6},{5,7},{6,4},{7,5},{8,10},{9,11},{10,... | collective-permute-start | bytes 3080 | tf_op jit(solution)/shard_map/ppermute | solution.py:19
  41.8 17.6 %collective-permute-start.22 = (f32[8,32]{1,0:T(8,128)S(1)}, f32[8,32]{1,0:T(8,128)}, u32[]{:S(2)}, u32[]{:S(2)}) collective-permute-start(f32[8,32]{1,0:T(8,128)S(1)} %bitcast.64), channel_id=1, source_target_pairs={{0,3},{1,0},{2,1},{3,2},{4,7},{5,4},{6,5},{7,6},{8,11},{9,8},{10,9... | collective-permute-start | bytes 3080 | tf_op jit(solution)/shard_map/ppermute | solution.py:19
  55.0 8.5 %copy-start.17 = (s32[128]{0:T(128)S(1)}, s32[128]{0:T(128)}, u32[]{:S(2)}) copy-start(s32[128]{0:T(128)} %and_select_fusion.1) | copy-start | bytes 1540
  56.3 7.0 %copy-start.18 = (s32[256]{0:T(256)S(1)}, s32[256]{0:T(256)}, u32[]{:S(2)}) copy-start(s32[256]{0:T(256)} %and_select_fusion.5) | copy-start | bytes 3076
  57.6 6.2 %collective-permute-start.6 = (f32[32,8,128]{2,1,0:T(8,128)}, f32[32,8,128]{2,1,0:T(8,128)S(1)}, u32[]{:S(2)}, u32[]{:S(2)}) collective-permute-start(f32[32,8,128]{2,1,0:T(8,128)} %get-tuple-element.84), channel_id=1, source_target_pairs={{0,4},{4,8},{8,12},{12,0},{1,5},{5,9},{9,13},{13,1},{2,6},{6,10},{... | collective-permute-start | bytes 393224 | tf_op jit(solution)/shard_map/ppermute | solution.py:19
  57.6 9.9 %collective-permute-start.7 = (f32[32,8,128]{2,1,0:T(8,128)S(1)}, f32[32,8,128]{2,1,0:T(8,128)S(1)}, u32[]{:S(2)}, u32[]{:S(2)}) collective-permute-start(f32[32,8,128]{2,1,0:T(8,128)S(1)} %get-tuple-element.83), channel_id=1, source_target_pairs={{0,12},{4,0},{8,4},{12,8},{1,13},{5,1},{9,5},{13,9},{2,14},{6,2},{... | collective-permute-start | bytes 393224 | tf_op jit(solution)/shard_map/ppermute | solution.py:19
  59.4 79.6 %collective-permute-start = (f32[8,256,128]{1,2,0:T(8,128)}, f32[8,256,128]{1,2,0:T(8,128)}, u32[]{:S(2)}, u32[]{:S(2)}) collective-permute-start(f32[8,256,128]{1,2,0:T(8,128)} %copy.55), channel_id=1, source_target_pairs={{0,1},{1,2},{2,3},{3,0},{4,5},{5,6},{6,7},{7,4},{8,9},{9,10},{10,1... | collective-permute-start | bytes 3145736 | tf_op jit(solution)/shard_map/ppermute | solution.py:19
  63.5 9.4 %copy-start.6 = (f32[16,128,64]{2,1,0:T(8,128)S(1)}, f32[16,128,64]{2,1,0:T(8,128)}, u32[]{:S(2)}) copy-start(f32[16,128,64]{2,1,0:T(8,128)} %shard_map.39) | copy-start | bytes 1572868
  63.8 77.2 %collective-permute-start.1 = (f32[8,256,128]{1,2,0:T(8,128)}, f32[8,256,128]{1,2,0:T(8,128)}, u32[]{:S(2)}, u32[]{:S(2)}) collective-permute-start(f32[8,256,128]{1,2,0:T(8,128)} %copy.56), channel_id=1, source_target_pairs={{0,3},{1,0},{2,1},{3,2},{4,7},{5,4},{6,5},{7,6},{8,11},{9,8},{10,9... | collective-permute-start | bytes 3145736 | tf_op jit(solution)/shard_map/ppermute | solution.py:19
  68.7 21.8 %collective-permute-start.8 = (f32[32,8,272]{2,1,0:T(8,128)}, f32[32,8,272]{2,1,0:T(8,128)}, u32[]{:S(2)}, u32[]{:S(2)}) collective-permute-start(f32[32,8,272]{2,1,0:T(8,128)} %maximum_bitcast_fusion), channel_id=1, source_target_pairs={{0,16},{16,0},{1,17},{17,1},{2,18},{18,2},{3,19},{19,3},{4,20},{20... | collective-permute-start | bytes 835592 | tf_op jit(solution)/shard_map/ppermute | solution.py:19
  72.9 1.9 copy-start.8
  72.9 1.9 copy-start.13
  72.9 1.8 copy-start.14
  73.0 4.6 %collective-permute-start.12 = (f32[32,8,64]{2,1,0:T(8,128)S(1)}, f32[32,8,64]{2,1,0:T(8,128)S(1)}, u32[]{:S(2)}, u32[]{:S(2)}) collective-permute-start(f32[32,8,64]{2,1,0:T(8,128)S(1)} %get-tuple-element.89), channel_id=1, source_target_pairs={{0,4},{4,8},{8,12},{12,0},{1,5},{5,9},{9,13},{13,1},{2,6},{6,10},{... | collective-permute-start | bytes 196616 | tf_op jit(solution)/shard_map/ppermute | solution.py:19
  73.0 6.1 %collective-permute-start.13 = (f32[32,8,64]{2,1,0:T(8,128)S(1)}, f32[32,8,64]{2,1,0:T(8,128)S(1)}, u32[]{:S(2)}, u32[]{:S(2)}) collective-permute-start(f32[32,8,64]{2,1,0:T(8,128)S(1)} %get-tuple-element.90), channel_id=1, source_target_pairs={{0,12},{4,0},{8,4},{12,8},{1,13},{5,1},{9,5},{13,9},{2,14},{6,2},{... | collective-permute-start | bytes 196616 | tf_op jit(solution)/shard_map/ppermute | solution.py:19
  77.6 1.5 copy-start.9
  77.6 14.3 %collective-permute-start.9 = (f32[32,8,272]{2,1,0:T(8,128)}, f32[32,8,272]{2,1,0:T(8,128)}, u32[]{:S(2)}, u32[]{:S(2)}) collective-permute-start(f32[32,8,272]{2,1,0:T(8,128)} %maximum_bitcast_fusion.1), channel_id=1, source_target_pairs={{0,16},{16,0},{1,17},{17,1},{2,18},{18,2},{3,19},{19,3},{4,20},{20... | collective-permute-start | bytes 835592 | tf_op jit(solution)/shard_map/ppermute | solution.py:19
  79.1 0.7 copy-start.11
  86.4 30.8 %collective-permute-start.14 = (f32[32,8,144]{2,1,0:T(8,128)}, f32[32,8,144]{2,1,0:T(8,128)}, u32[]{:S(2)}, u32[]{:S(2)}) collective-permute-start(f32[32,8,144]{2,1,0:T(8,128)} %copy.47), channel_id=1, source_target_pairs={{0,16},{16,0},{1,17},{17,1},{2,18},{18,2},{3,19},{19,3},{4,20},{20... | collective-permute-start | bytes 442376 | tf_op jit(solution)/shard_map/ppermute | solution.py:19
  90.5 29.9 %collective-permute-start.15 = (f32[32,8,144]{2,1,0:T(8,128)}, f32[32,8,144]{2,1,0:T(8,128)}, u32[]{:S(2)}, u32[]{:S(2)}) collective-permute-start(f32[32,8,144]{2,1,0:T(8,128)} %copy.49), channel_id=1, source_target_pairs={{0,16},{16,0},{1,17},{17,1},{2,18},{18,2},{3,19},{19,3},{4,20},{20... | collective-permute-start | bytes 442376 | tf_op jit(solution)/shard_map/ppermute | solution.py:19
  93.0 2.2 %copy-start.1 = (f32[32,256,128]{2,1,0:T(8,128)S(1)}, f32[32,256,128]{2,1,0:T(8,128)}, u32[]{:S(2)}) copy-start(f32[32,256,128]{2,1,0:T(8,128)} %c_ref.3) | copy-start | bytes 12582916
  114.0 3.2 %copy-start.2 = (f32[2,32,256,128]{3,2,1,0:T(8,128)}, f32[2,32,256,128]{3,2,1,0:T(8,128)S(1)}, u32[]{:S(2)}) copy-start(f32[2,32,256,128]{3,2,1,0:T(8,128)S(1)} %shard_map.38.g_ref) | copy-start | bytes 25165828
  117.2 6.3 %copy-start.10 = (f32[32,8,64]{2,1,0:T(8,128)S(1)}, f32[32,8,64]{2,1,0:T(8,128)}, u32[]{:S(2)}) copy-start(f32[32,8,64]{2,1,0:T(8,128)} %copy-done.9) | copy-start | bytes 196612
  117.2 6.3 %copy-start.12 = (f32[32,8,64]{2,1,0:T(8,128)S(1)}, f32[32,8,64]{2,1,0:T(8,128)}, u32[]{:S(2)}) copy-start(f32[32,8,64]{2,1,0:T(8,128)} %copy-done.11) | copy-start | bytes 196612
  138.9 5.3 %copy-start.4 = (f32[16,256,128]{2,1,0:T(8,128)}, f32[16,256,128]{2,1,0:T(8,128)S(1)}, u32[]{:S(2)}) copy-start(f32[16,256,128]{2,1,0:T(8,128)S(1)} %shard_map.40.e_ref) | copy-start | bytes 6291460
  142.3 2.0 %copy-start.7 = (f32[16,256,128]{1,2,0:T(8,128)}, f32[16,256,128]{1,2,0:T(8,128)S(1)}, u32[]{:S(2)}) copy-start(f32[16,256,128]{1,2,0:T(8,128)S(1)} %constant_dynamic-update-slice_fusion) | copy-start | bytes 6291460
  144.3 10.7 %copy-start.5 = (f32[16,256,128]{2,1,0:T(8,128)S(1)}, f32[16,256,128]{2,1,0:T(8,128)}, u32[]{:S(2)}) copy-start(f32[16,256,128]{2,1,0:T(8,128)} %copy-done.4) | copy-start | bytes 6291460
  145.9 4.3 %collective-permute-start.2 = (f32[16,8,128]{2,1,0:T(8,128)S(1)}, f32[16,8,128]{2,1,0:T(8,128)S(1)}, u32[]{:S(2)}, u32[]{:S(2)}) collective-permute-start(f32[16,8,128]{2,1,0:T(8,128)S(1)} %copy.34), channel_id=1, source_target_pairs={{0,4},{4,8},{8,12},{12,0},{1,5},{5,9},{9,13},{13,1},{2,6},{6,10},{... | collective-permute-start | bytes 196616 | tf_op jit(solution)/shard_map/ppermute | solution.py:19
  148.5 3.7 %collective-permute-start.3 = (f32[16,8,128]{2,1,0:T(8,128)S(1)}, f32[16,8,128]{2,1,0:T(8,128)S(1)}, u32[]{:S(2)}, u32[]{:S(2)}) collective-permute-start(f32[16,8,128]{2,1,0:T(8,128)S(1)} %copy.35), channel_id=1, source_target_pairs={{0,12},{4,0},{8,4},{12,8},{1,13},{5,1},{9,5},{13,9},{2,14},{6,2},{... | collective-permute-start | bytes 196616 | tf_op jit(solution)/shard_map/ppermute | solution.py:19
  152.5 19.8 %collective-permute-start.4 = (f32[16,8,272]{2,1,0:T(8,128)S(1)}, f32[16,8,272]{2,1,0:T(8,128)}, u32[]{:S(2)}, u32[]{:S(2)}) collective-permute-start(f32[16,8,272]{2,1,0:T(8,128)S(1)} %maximum_bitcast_fusion.2), channel_id=1, source_target_pairs={{0,16},{16,0},{1,17},{17,1},{2,18},{18,2},{3,19},{19,3},{4,20},{20... | collective-permute-start | bytes 417800 | tf_op jit(solution)/shard_map/ppermute | solution.py:19
  153.5 18.8 %collective-permute-start.5 = (f32[16,8,272]{2,1,0:T(8,128)S(1)}, f32[16,8,272]{2,1,0:T(8,128)}, u32[]{:S(2)}, u32[]{:S(2)}) collective-permute-start(f32[16,8,272]{2,1,0:T(8,128)S(1)} %maximum_bitcast_fusion.3), channel_id=1, source_target_pairs={{0,16},{16,0},{1,17},{17,1},{2,18},{18,2},{3,19},{19,3},{4,20},{20... | collective-permute-start | bytes 417800 | tf_op jit(solution)/shard_map/ppermute | solution.py:19
  154.9 3.4 %copy-start.3 = (f32[2,32,256,128]{3,2,1,0:T(8,128)S(1)}, f32[2,32,256,128]{3,2,1,0:T(8,128)}, u32[]{:S(2)}) copy-start(f32[2,32,256,128]{3,2,1,0:T(8,128)} %copy-done.2) | copy-start | bytes 25165828
